TPU v7x, 32 devices: a whole 2x2x4 slice. The times are simulated.
32 devices in a mesh: sec: 2 (over core), dp: 4 (over y, x), tp: 4 (over z).
Axes of the slice: x: 2, y: 2, z: 4, core: 2. Of those that a mesh axis runs over, the one named last changes fastest.
Arguments:
- feats: bfloat16 [2, 512, 1280], P('sec', 'dp'), may hold values from -6 to 6
- dest: int32 [2, 512, 1], P('sec', 'dp'), may hold values from 0 to 3; in each aligned block of 128 rows (0 to 127, 128 to 255, ..., all dimensions but the last counted through in order) at most 64 rows name the same one
- proj_w: bfloat16 [1280, 8192], P(('sec', 'dp'), 'tp'), may hold values from -0.15625 to 0.15625
- proj_b: bfloat16 [8192], P('tp'), may hold values from -3 to 3
- text: bfloat16 [2, 1024, 8192], P('sec', 'dp', 'tp'), may hold values from -6 to 6
- gain: bfloat16 [8192], P('tp'), may hold values from 0.5 to 1.5
- cot: bfloat16 [2, 1024, 8192], P('sec', 'dp', 'tp'), may hold values from -6 to 6
Outputs:
- normed: bfloat16 [2, 1024, 8192], P('sec', 'dp', 'tp')
- feature_grad: bfloat16 [2, 512, 1280], P('sec', 'dp')
Inputs may be any that keep to these rules, and one draw needn't show every extreme that they name: `dest`: among the 128 tokens of one dp index in one micro-batch, no target is named more than 64 times, a bound that some block reaches.
All inputs are finite; a program needn't handle non-finite values.
Results may differ from a plain program's by a relative error of at most 0.005.
Values may be sent and summed in bfloat16 or wider, within the bound.
A program may use at most 64 MiB of HBM per device.

v0:
```python
import jax
import jax.numpy as jnp
from jax import lax
from jax.sharding import PartitionSpec as P


def from_behind(value, axis, steps):
    count = lax.axis_size(axis)
    pairs = [(source, (source + steps) % count) for source in range(count)]
    return lax.ppermute(value, axis, pairs)


def route_forward(outgoing):
    regrouped = lax.all_to_all(outgoing, "dp", split_axis=0, concat_axis=0, tiled=True)
    return from_behind(regrouped, "sec", 1)


def route_backward(incoming):
    hopped = from_behind(incoming, "sec", -1)
    return lax.all_to_all(hopped, "dp", split_axis=0, concat_axis=0, tiled=True)


def body(feats, dest, proj_w, proj_b, text, gain, cot):
    rows_in = feats[0]
    per_device = rows_in.shape[0]
    group_size = lax.axis_size("dp")
    tp_size = lax.axis_size("tp")
    capacity = 2 * per_device // group_size
    slot_total = group_size * capacity
    weight = lax.all_gather(proj_w, ("sec", "dp"), axis=0, tiled=True)
    target = dest[0, :, 0]
    lanes = jnp.arange(group_size, dtype=jnp.int32)
    onehot = (target[:, None] == lanes[None, :]).astype(jnp.int32)
    before = jnp.cumsum(onehot, axis=0) - onehot
    position = jnp.sum(before * onehot, axis=1)
    slot_index = target * capacity + position
    placer = (jnp.arange(slot_total, dtype=jnp.int32)[:, None] == slot_index[None, :]).astype(
        jnp.bfloat16
    )
    bias_wide = proj_b.astype(jnp.float32)
    counts = jnp.sum(onehot, axis=0).reshape(group_size, 1)
    counts_moved = lax.all_to_all(counts, "dp", split_axis=0, concat_axis=0, tiled=True)
    counts_in = from_behind(counts_moved, "sec", 1)
    occupied = (jnp.arange(capacity, dtype=jnp.int32)[None, :] < counts_in).reshape(slot_total, 1)
    projected = (jnp.dot(rows_in, weight, preferred_element_type=jnp.float32) + bias_wide).astype(
        jnp.bfloat16
    )
    outgoing = jnp.dot(placer, projected, preferred_element_type=jnp.float32).astype(jnp.bfloat16)
    arrived = route_forward(outgoing.reshape(group_size, capacity, -1))
    packed = arrived.reshape(slot_total, -1)
    gain_wide = gain.astype(jnp.float32)
    hidden = jnp.where(occupied, packed.astype(jnp.float32), text[0].astype(jnp.float32))
    scaled = cot[0].astype(jnp.float32) * gain_wide
    squares, cross = lax.psum(
        (jnp.sum(hidden * hidden, axis=1), jnp.sum(scaled * hidden, axis=1)), "tp"
    )
    full_width = hidden.shape[1] * tp_size
    inverse = lax.rsqrt(squares / full_width + 1e-05)
    normed = (hidden * inverse[:, None] * gain_wide).astype(jnp.bfloat16)
    grad_hidden = (
        inverse[:, None] * scaled
        - hidden * (inverse * inverse * inverse * cross / full_width)[:, None]
    ).astype(jnp.bfloat16)
    returned = route_backward(grad_hidden.reshape(group_size, capacity, -1)).reshape(slot_total, -1)
    grad_tokens = jnp.dot(placer.T, returned, preferred_element_type=jnp.float32).astype(
        jnp.bfloat16
    )
    partial_value = lax.dot_general(
        grad_tokens, weight, (((1,), (1,)), ((), ())), preferred_element_type=jnp.float32
    )
    feature_grad = lax.psum(partial_value, "tp").astype(jnp.bfloat16)
    return (normed[None], feature_grad[None])


def solution(mesh):
    in_specs = (
        P("sec", "dp", None),
        P("sec", "dp", None),
        P(("sec", "dp"), "tp"),
        P("tp"),
        P("sec", "dp", "tp"),
        P("tp"),
        P("sec", "dp", "tp"),
    )
    out_specs = (P("sec", "dp", "tp"), P("sec", "dp", None))
    return jax.shard_map(body, mesh=mesh, in_specs=in_specs, out_specs=out_specs, check_vma=False)
```

profile of v0, /device:TPU:0, one launch (start us, length us, event | category | flops | bytes accessed | tf_op | source)
XLA Modules:
  0.0 163.8 jit_solution(10700266229924291600)
XLA Ops:
  7.2 0.0 copy-start
  7.2 0.0 all-gather.2.cloned.1.call-start
  7.2 0.7 all-gather.2.cloned.1.call-update
  7.9 0.7 convert_element_type.81
  8.6 0.7 fusion.13
  9.3 0.2 reduce_window_sum.11
  9.5 0.8 fusion.14
  10.3 0.7 multiply_add_fusion
  11.0 42.7 %all-gather.2.cloned.1.call-done = bf16[1280,2048]{1,0:T(8,128)(2,1)} async-done(((bf16[160,2048]{1,0:T(8,128)(2,1)}), bf16[1280,2048]{1,0:T(8,128)(2,1)}) %all-gather.2.cloned.1.call-update) | async-done | bytes 5242896 | tf_op jit(solution)/shard_map/all_gather | solution.py:30
  53.7 0.0 copy-done
  53.7 3.6 %convolution_convert_fusion = bf16[256,2048]{1,0:T(8,128)(2,1)S(1)} fusion(bf16[1280,2048]{1,0:T(8,128)(2,1)} %all-gather.2.cloned.1.call-done, f32[2048]{0:T(1024)S(1)} %convert_element_type.81, bf16[1,128,1280]{2,1,0:T(8,128)(2,1)S(1)} %copy-done, s32[128]{0:T(128)S(1)} %multiply_add_fusion), kind=kOutput, calls=%fused_computation | convolution fusion | flops 806387712 | bytes 6627840 | tf_op jit(solution)/shard_map/dot_general | solution.py:48
  57.4 0.0 copy-start.3
  57.4 0.0 copy-start.1
  57.4 17.4 %all_to_all.22 = bf16[4,64,2048]{2,1,0:T(8,128)(2,1)S(1)} all-to-all(bf16[4,64,2048]{2,1,0:T(8,128)(2,1)S(1)} %bitcast.46), channel_id=1, replica_groups=mesh['sec'=2,'dp'=4,'tp'=4] {'dp'}, dimensions={0} | all-to-all | bytes 2097152 | tf_op jit(solution)/shard_map/all_to_all | solution.py:14
  74.8 0.0 collective-permute-start.1
  74.8 0.7 copy.10
  75.5 3.2 %all-to-all-start = ((s32[4,1,1]{2,1,0:T(1,128)}), s32[4,1,1]{2,1,0:T(1,128)S(1)}, u32[]{:S(2)}, u32[]{:S(2)}) async-start(s32[4,1,1]{2,1,0:T(1,128)} %copy.10), calls=%async_computation | async-start | bytes 4096 | tf_op jit(solution)/shard_map/all_to_all | solution.py:42
  78.7 0.0 copy-done.3
  78.7 4.5 %all-to-all-done = s32[4,1,1]{2,1,0:T(1,128)S(1)} async-done(((s32[4,1,1]{2,1,0:T(1,128)}), s32[4,1,1]{2,1,0:T(1,128)S(1)}, u32[]{:S(2)}, u32[]{:S(2)}) %all-to-all-start) | async-done | bytes 48 | tf_op jit(solution)/shard_map/all_to_all | solution.py:42
  83.2 0.2 reduce.1
  83.4 0.1 collective-permute-start
  83.5 1.1 collective-permute-done
  84.6 0.1 iota_compare_fusion.5
  84.6 0.1 lt.27
  84.7 0.0 collective-permute-done.1
  84.7 0.0 copy-done.1
  84.7 0.0 copy-start.2
  84.7 1.8 %multiply_reduce_fusion = (f32[4,64]{1,0:T(4,128)S(1)}, f32[4,64,2048]{2,1,0:T(8,128)}) fusion(pred[4,64]{1,0:T(4,128)(4,1)S(1)} %iota_compare_fusion.5, bf16[4,64,2048]{2,1,0:T(8,128)(2,1)S(1)} %collective-permute-done.1, bf16[4,64,2048]{2,1,0:T(8,128)(2,1)S(1)} %bitcast.42), kind=kLoop, calls=%fused_computation.13 | loop fusion | flops 2621184 | bytes 4195584 | tf_op jit(solution)/shard_map/reduce_sum | solution.py:55
  86.5 0.1 reduce_sum.41
  86.6 0.0 copy-done.2
  86.6 0.6 fusion.2
  87.2 11.7 %all-reduce = (f32[256]{0:T(256)S(1)}, f32[256]{0:T(256)S(1)}) all-reduce(f32[256]{0:T(256)S(1)} %reduce_sum.41, f32[256]{0:T(256)S(1)} %fusion.2), channel_id=1, replica_groups=mesh['sec'=2,'dp'=4,'tp'=4] {'tp'}, use_global_device_ids=true, to_apply=%region_4.5 | all-reduce | flops 512 | bytes 4096 | tf_op jit(solution)/shard_map/psum | solution.py:54
  98.9 0.1 mul.90
  99.0 0.1 mul.101
  99.1 2.2 %subtract_convert_fusion = bf16[4,64,2048]{2,1,0:T(8,128)(2,1)S(1)} fusion(f32[4,64]{1,0:T(4,128)S(1)} %mul.101, f32[2048]{0:T(1024)S(1)} %convert_element_type.90, f32[4,64]{1,0:T(4,128)S(1)} %mul.90, f32[4,64,2048]{2,1,0:T(8,128)} %get-tuple-element.7, pred[4,64]{1,0:T(4,128)(4,1)S(1)} %iota_compare_fusion.5, ...), kind=kLoop, calls=%fused_computation.12 | loop fusion | flops 4194304 | bytes 5253376 | tf_op jit(solution)/shard_map/convert_element_type | solution.py:63
  101.2 0.1 collective-permute-start.2
  101.3 2.8 %collective-permute-done.2 = bf16[4,64,2048]{2,1,0:T(8,128)(2,1)} collective-permute-done((bf16[4,64,2048]{2,1,0:T(8,128)(2,1)S(1)}, bf16[4,64,2048]{2,1,0:T(8,128)(2,1)}, u32[]{:S(2)}, u32[]{:S(2)}) %collective-permute-start.2) | collective-permute-done | bytes 1048608 | tf_op jit(solution)/shard_map/ppermute | solution.py:10
  104.1 3.5 %all-to-all-start.2 = ((bf16[4,64,2048]{2,1,0:T(8,128)(2,1)}), bf16[4,64,2048]{2,1,0:T(8,128)(2,1)S(1)}, u32[]{:S(2)}, u32[]{:S(2)}) async-start(bf16[4,64,2048]{2,1,0:T(8,128)(2,1)} %collective-permute-done.2), calls=%async_computation.2 | async-start | bytes 2097152 | tf_op jit(solution)/shard_map/all_to_all | solution.py:20
  107.6 0.2 convert_element_type.103
  107.9 1.4 fusion.5
  109.3 12.6 %all-to-all-done.2 = bf16[4,64,2048]{2,1,0:T(8,128)(2,1)S(1)} async-done(((bf16[4,64,2048]{2,1,0:T(8,128)(2,1)}), bf16[4,64,2048]{2,1,0:T(8,128)(2,1)S(1)}, u32[]{:S(2)}, u32[]{:S(2)}) %all-to-all-start.2) | async-done | bytes 1048608 | tf_op jit(solution)/shard_map/all_to_all | solution.py:20
  121.8 4.4 %fusion.6 = f32[128,1280]{1,0:T(8,128)S(1)} fusion(bf16[1280,2048]{1,0:T(8,128)(2,1)} %all-gather.2.cloned.1.call-done, bf16[256,2048]{1,0:T(8,128)(2,1)S(1)} %bitcast.45, s32[128]{0:T(128)S(1)} %multiply_add_fusion), kind=kOutput, calls=%fused_computation.14 | convolution fusion | flops 805601280 | bytes 6947328 | tf_op jit(solution)/shard_map/dot_general | solution.py:68
  126.2 30.8 %all-reduce.2 = bf16[128,1280]{1,0:T(8,128)(2,1)} all-reduce(f32[128,1280]{1,0:T(8,128)S(1)} %fusion.6), channel_id=1, replica_groups=mesh['sec'=2,'dp'=4,'tp'=4] {'tp'}, use_global_device_ids=true, to_apply=%region_7.8 | all-reduce | flops 163840 | bytes 983040 | tf_op jit(solution)/shard_map/psum | solution.py:71
  (2 shorter events, 0.0 us)
Async XLA Ops:
  7.2 46.6 %copy-start = (bf16[1,128,1280]{2,1,0:T(8,128)(2,1)S(1)}, bf16[1,128,1280]{2,1,0:T(8,128)(2,1)}, u32[]{:S(2)}) copy-start(bf16[1,128,1280]{2,1,0:T(8,128)(2,1)} %param.7) | copy-start | bytes 983044
  7.2 46.6 %all-gather.2.cloned.1.call-start = ((), (), s32[]{:S(2)}) async-start(), calls=%async_computation.3 | async-start | bytes 5898240 | tf_op jit(solution)/shard_map/all_gather | solution.py:30
  57.4 21.3 %copy-start.3 = (bf16[2048]{0:T(1024)(128)(2,1)S(1)}, bf16[2048]{0:T(1024)(128)(2,1)}, u32[]{:S(2)}) copy-start(bf16[2048]{0:T(1024)(128)(2,1)} %param.12) | copy-start | bytes 12292
  57.4 27.4 %copy-start.1 = (bf16[1,256,2048]{2,1,0:T(8,128)(2,1)S(1)}, bf16[1,256,2048]{2,1,0:T(8,128)(2,1)}, u32[]{:S(2)}) copy-start(bf16[1,256,2048]{2,1,0:T(8,128)(2,1)} %param.11) | copy-start | bytes 3145732
  74.8 9.9 %collective-permute-start.1 = (bf16[4,64,2048]{2,1,0:T(8,128)(2,1)S(1)}, bf16[4,64,2048]{2,1,0:T(8,128)(2,1)S(1)}, u32[]{:S(2)}, u32[]{:S(2)}) collective-permute-start(bf16[4,64,2048]{2,1,0:T(8,128)(2,1)S(1)} %all_to_all.22), channel_id=1, source_target_pairs={{0,16},{16,0},{1,17},{17,1},{2,18},{18,2},{3,19},{19,3},{4,20},{20... | collective-permute-start | bytes 3145736 | tf_op jit(solution)/shard_map/ppermute | solution.py:10
  75.5 7.8 %all-to-all-start = ((s32[4,1,1]{2,1,0:T(1,128)}), s32[4,1,1]{2,1,0:T(1,128)S(1)}, u32[]{:S(2)}, u32[]{:S(2)}) async-start(s32[4,1,1]{2,1,0:T(1,128)} %copy.10), calls=%async_computation | async-start | bytes 4096 | tf_op jit(solution)/shard_map/all_to_all | solution.py:42
  83.4 1.2 collective-permute-start
  84.7 1.8 %copy-start.2 = (bf16[1,256,2048]{2,1,0:T(8,128)(2,1)S(1)}, bf16[1,256,2048]{2,1,0:T(8,128)(2,1)}, u32[]{:S(2)}) copy-start(bf16[1,256,2048]{2,1,0:T(8,128)(2,1)} %param.13) | copy-start | bytes 3145732
  101.2 2.9 %collective-permute-start.2 = (bf16[4,64,2048]{2,1,0:T(8,128)(2,1)S(1)}, bf16[4,64,2048]{2,1,0:T(8,128)(2,1)}, u32[]{:S(2)}, u32[]{:S(2)}) collective-permute-start(bf16[4,64,2048]{2,1,0:T(8,128)(2,1)S(1)} %subtract_convert_fusion), channel_id=1, source_target_pairs={{0,16},{16,0},{1,17},{17,1},{2,18},{18,2},{3,19},{19,3},{4,20},{20... | collective-permute-start | bytes 3145736 | tf_op jit(solution)/shard_map/ppermute | solution.py:10
  104.1 17.7 %all-to-all-start.2 = ((bf16[4,64,2048]{2,1,0:T(8,128)(2,1)}), bf16[4,64,2048]{2,1,0:T(8,128)(2,1)S(1)}, u32[]{:S(2)}, u32[]{:S(2)}) async-start(bf16[4,64,2048]{2,1,0:T(8,128)(2,1)} %collective-permute-done.2), calls=%async_computation.2 | async-start | bytes 2097152 | tf_op jit(solution)/shard_map/all_to_all | solution.py:20
Sparse Core Ops, SparseCore 0:
  9.9 43.8 all-gather.1
where the time goes:
time: 164 us
  waiting for transfers between devices  64.4 us (39%)
  blocking collectives  59.9 us (37%)
  between operations  14.2 us (9%)
  other arithmetic  9.5 us (6%)
  matrix products  7.98 us (5%)
  starting transfers between devices  6.92 us (4%)
    all_gather x1, waiting for transfers between devices, body(): weight = lax.all_gather(proj_w, ('sec', 'dp'), axis=0, tiled=True)  42.7 us
    psum x1, blocking collectives, body(): feature_grad = lax.psum(partial_value, 'tp').astype(jnp.bfloat16)  30.8 us
    all_to_all x1, blocking collectives, route_forward(): lax.all_to_all(outgoing, 'dp', split_axis=0, concat_axis=0, tiled=True)  17.4 us
    all_to_all x1, waiting for transfers between devices, route_backward(): return lax.all_to_all(hopped, 'dp', split_axis=0, concat_axis=0, tiled=True)  12.6 us
    psum x1, blocking collectives, body(): lax.psum((jnp.sum(hidden * hidden, axis=1), jnp.sum(scaled * hidden, axis...  11.7 us
    all_to_all x1, waiting for transfers between devices, body(): lax.all_to_all(counts, 'dp', split_axis=0, concat_axis=0, tiled=True)  4.52 us
    dot_general x1, matrix products, body(): lax.dot_general(grad_tokens, weight, (((1,), (1,)), ((), ())), preferred_...  4.37 us
    ppermute x3, waiting for transfers between devices, from_behind(): return lax.ppermute(value, axis, pairs)  3.89 us
  transfers between devices with their start and end apart: 6, of which 5 were waited for; matrix products, arithmetic and copies ran while one was open for 3% of the time, Pallas kernels for 0%

commit v1 on v0

--- a/solution.py
+++ b/solution.py
@@ -1,6 +1,10 @@
+import functools
+
 import jax
 import jax.numpy as jnp
 from jax import lax
+from jax.experimental import pallas as pl
+from jax.experimental.pallas import tpu as pltpu
 from jax.sharding import PartitionSpec as P
 
 
@@ -72,6 +76,309 @@
     return (normed[None], feature_grad[None])
 
 
+MESH = pl.DeviceIdType.MESH
+FLAG = 128
+CHUNKS = 8
+AHEAD = 3
+PARTS = 5
+
+
+def kernel(
+    feats_ref, dest_ref, shard_ref, bias_ref, text_hbm, gain_ref, cot_hbm,
+    normed_ref, grad_ref,
+    weight, text, cot, outbox, slots, hidden, grad, product, returned, tokens, partial, result, stats,
+    local_sem, w_send, w_recv, x_send, x_recv, y_send, y_recv, s_send, s_recv,
+    p_send, p_recv, r_send, r_recv, g_send, g_recv,
+):
+    sec, dp, tp = lax.axis_index("sec"), lax.axis_index("dp"), lax.axis_index("tp")
+    other = 1 - sec
+    x_dp = dp + 1 - 2 * lax.rem(dp, 2)
+    y_dp = lax.rem(dp + 2, 4)
+    d_dp = 3 - dp
+    per_device, vision = feats_ref.shape
+    depth, width = shard_ref.shape
+    n_dp, n_tp, quarter, _ = slots.shape
+    cap = n_tp * quarter
+    rows = n_dp * cap
+    cw = width // CHUNKS
+    pw = vision // PARTS
+    tok_q = per_device // n_tp
+    half = depth // 2
+
+    def block(sec_of, dp_of):
+        return pl.multiple_of((sec_of * n_dp + dp_of) * depth, 16)
+
+    own = block(sec, dp)
+    local = [
+        pltpu.make_async_copy(shard_ref, weight.at[pl.ds(own, depth)], local_sem.at[0]),
+        pltpu.make_async_copy(text_hbm, text, local_sem.at[1]),
+        pltpu.make_async_copy(cot_hbm, cot, local_sem.at[2]),
+    ]
+    for copy in local:
+        copy.start()
+
+    barrier = pltpu.get_barrier_semaphore()
+    peers = [(sec, x_dp, tp), (sec, y_dp, tp), (sec, d_dp, tp)]
+    peers += [(other, dp, tp), (other, x_dp, tp), (other, y_dp, tp), (other, d_dp, tp)]
+    peers += [(sec, dp, lax.rem(tp + k, n_tp)) for k in range(1, n_tp)]
+    for peer in peers:
+        pl.semaphore_signal(barrier, inc=1, device_id=peer, device_id_type=MESH)
+
+    t_col = dest_ref[...].astype(jnp.float32)
+    square = (per_device, per_device)
+    down = lax.broadcasted_iota(jnp.int32, square, 0)
+    along = lax.broadcasted_iota(jnp.int32, square, 1)
+    t_row = jnp.sum(jnp.where(down == along, t_col, 0.0), axis=0, keepdims=True)
+    same = t_col == t_row
+    before_row = jnp.sum(jnp.where(same & (down < along), 1.0, 0.0), axis=0, keepdims=True)
+    before_col = jnp.sum(jnp.where(same & (along < down), 1.0, 0.0), axis=1, keepdims=True)
+    slot_row = (t_row * cap + before_row).astype(jnp.int32)
+    slot_col = (t_col * cap + before_col).astype(jnp.int32)
+    mine = lax.broadcasted_iota(jnp.int32, (n_dp * quarter, per_device), 0)
+    mine = mine + (mine // quarter) * (cap - quarter) + tp * quarter
+    placer = jnp.where(mine == slot_row, 1.0, 0.0)
+    filled = jnp.broadcast_to(jnp.sum(placer, axis=1, keepdims=True), (n_dp * quarter, FLAG))
+    routed = jnp.dot(placer.astype(jnp.bfloat16), feats_ref[...], preferred_element_type=jnp.float32)
+    outbox[:, :, pl.ds(0, vision)] = routed.astype(jnp.bfloat16).reshape(n_dp, quarter, vision)
+    outbox[:, :, pl.ds(vision, FLAG)] = filled.astype(jnp.bfloat16).reshape(n_dp, quarter, FLAG)
+    unplacer = jnp.where(
+        slot_col == lax.broadcasted_iota(jnp.int32, (per_device, rows), 1), 1.0, 0.0
+    ).astype(jnp.bfloat16)
+
+    def remote(src, dst, send, recv, device):
+        return pltpu.make_async_remote_copy(
+            src_ref=src, dst_ref=dst, send_sem=send, recv_sem=recv,
+            device_id=device, device_id_type=MESH,
+        )
+
+    sent = []
+
+    def start(copy):
+        copy.start()
+        sent.append(copy)
+
+    def w_copy(first, count, chunk, kind, device):
+        ref = weight.at[pl.ds(first, count), pl.ds(chunk * cw, cw)]
+        return remote(ref, ref, w_send.at[chunk, kind], w_recv.at[chunk, kind], device)
+
+    to_x, to_y, to_sib = (sec, x_dp, tp), (sec, y_dp, tp), (other, dp, tp)
+    jx, jy, jd = block(sec, x_dp), block(sec, y_dp), block(sec, d_dp)
+    jd_low = pl.multiple_of(jd + half, 16)
+    jy_low = pl.multiple_of(jy + half, 16)
+    sib = [block(other, k) for k in (dp, x_dp, y_dp, d_dp)]
+
+    def send_own(chunk):
+        start(w_copy(own, depth, chunk, 0, to_x))
+        start(w_copy(own, depth, chunk, 1, to_y))
+        start(w_copy(own, depth, chunk, 4, to_sib))
+
+    local[0].wait()
+    pl.semaphore_wait(barrier, len(peers))
+
+    for to in (d_dp, x_dp, y_dp, dp):
+        start(remote(outbox.at[to], slots.at[dp, tp], x_send.at[to], x_recv.at[dp], (other, to, tp)))
+    for chunk in range(AHEAD):
+        send_own(chunk)
+    for source in range(n_dp):
+        remote(outbox.at[source], slots.at[source, tp], x_send.at[source], x_recv.at[source], to_sib).wait_recv()
+    for k in range(1, n_tp):
+        to = lax.rem(tp + k, n_tp)
+        start(remote(slots.at[:, tp], slots.at[:, tp], y_send.at[k], y_recv.at[tp], (sec, dp, to)))
+
+    def project(chunk, square_sum, cross_sum):
+        cols = pl.ds(chunk * cw, cw)
+        value = jnp.dot(
+            slots[:, :, :, pl.ds(0, vision)].reshape(rows, vision),
+            weight[:, cols],
+            preferred_element_type=jnp.float32,
+        )
+        value = (value + bias_ref[:, cols].astype(jnp.float32)).astype(jnp.bfloat16)
+        flag = slots[:, :, :, pl.ds(vision, FLAG)].reshape(rows, FLAG).astype(jnp.float32)
+        flag = jnp.concatenate([flag] * (cw // FLAG), axis=1)
+        hid = jnp.where(flag > 0.5, value.astype(jnp.float32), text[:, cols].astype(jnp.float32))
+        hidden[:, cols] = hid.astype(jnp.bfloat16)
+        scaled = cot[:, cols].astype(jnp.float32) * gain_ref[:, cols].astype(jnp.float32)
+        for first in range(0, cw, 128):
+            part = hid[:, first:first + 128]
+            square_sum = square_sum + part * part
+            cross_sum = cross_sum + part * scaled[:, first:first + 128]
+        return square_sum, cross_sum
+
+    square_sum = jnp.zeros((rows, 128), jnp.float32)
+    cross_sum = jnp.zeros((rows, 128), jnp.float32)
+    for step in range(CHUNKS + 2):
+        if step < CHUNKS:
+            w_copy(jx, depth, step, 0, to_x).wait_recv()
+            start(w_copy(jx, half, step, 2, to_y))
+            w_copy(jy, depth, step, 1, to_y).wait_recv()
+            start(w_copy(jy_low, half, step, 3, to_x))
+            start(w_copy(jx, depth, step, 5, to_sib))
+            start(w_copy(jy, depth, step, 6, to_sib))
+            if step + AHEAD < CHUNKS:
+                send_own(step + AHEAD)
+        if 1 <= step <= CHUNKS:
+            w_copy(jd, half, step - 1, 2, to_y).wait_recv()
+            w_copy(jd_low, half, step - 1, 3, to_x).wait_recv()
+            start(w_copy(jd, depth, step - 1, 7, to_sib))
+        if step == 2:
+            for k in range(1, n_tp):
+                who = lax.rem(tp + k, n_tp)
+                remote(slots.at[:, who], slots.at[:, who], y_send.at[k], y_recv.at[who], to_sib).wait_recv()
+            local[1].wait()
+            local[2].wait()
+        if step >= 2:
+            for kind in range(4):
+                w_copy(sib[kind], depth, step - 2, 4 + kind, to_sib).wait_recv()
+            square_sum, cross_sum = project(step - 2, square_sum, cross_sum)
+
+    stats[tp, pl.ds(0, 1), :] = jnp.sum(square_sum.T, axis=0, keepdims=True)
+    stats[tp, pl.ds(1, 1), :] = jnp.sum(cross_sum.T, axis=0, keepdims=True)
+    for k in range(1, n_tp):
+        to = lax.rem(tp + k, n_tp)
+        start(remote(stats.at[tp], stats.at[tp], s_send.at[k], s_recv.at[tp], (sec, dp, to)))
+    for k in range(1, n_tp):
+        who = lax.rem(tp + k, n_tp)
+        remote(stats.at[who], stats.at[who], s_send.at[k], s_recv.at[who], to_sib).wait_recv()
+    total = stats[0] + stats[1] + stats[2] + stats[3]
+    full_width = width * n_tp
+    inverse = lax.rsqrt(total[0:1] / full_width + 1e-05)
+    factor = inverse * inverse * inverse * total[1:2] / full_width
+    inverse = jnp.broadcast_to(inverse, (128, rows)).T
+    factor = jnp.broadcast_to(factor, (128, rows)).T
+    inverse_wide = jnp.concatenate([inverse] * (cw // 128), axis=1)
+    factor_wide = jnp.concatenate([factor] * (cw // 128), axis=1)
+
+    for chunk in range(CHUNKS):
+        cols = pl.ds(chunk * cw, cw)
+        scaled = cot[:, cols].astype(jnp.float32) * gain_ref[:, cols].astype(jnp.float32)
+        hid = hidden[:, cols].astype(jnp.float32)
+        grad[:, cols] = (inverse_wide * scaled - hid * factor_wide).astype(jnp.bfloat16)
+
+    def p_copy(source, to, part, device):
+        cols = pl.ds(part * pw, pw)
+        return remote(
+            product.at[pl.ds(pl.multiple_of(to * cap, 16), cap), cols],
+            returned.at[pl.ds(pl.multiple_of(source * cap, 16), cap), cols],
+            p_send.at[part, to], p_recv.at[part, source], device,
+        )
+
+    for part in range(PARTS):
+        value = lax.dot_general(
+            grad[...], weight[pl.ds(part * pw, pw), :], (((1,), (1,)), ((), ())),
+            preferred_element_type=jnp.float32,
+        )
+        product[:, pl.ds(part * pw, pw)] = value.astype(jnp.bfloat16)
+        for to in (d_dp, x_dp, y_dp, dp):
+            start(p_copy(dp, to, part, (other, to, tp)))
+
+    def r_copy(owner, source, part, k, device):
+        cols = pl.ds(part * pw, pw)
+        return remote(
+            tokens.at[pl.ds(pl.multiple_of(owner * tok_q, 16), tok_q), cols],
+            partial.at[source, :, cols],
+            r_send.at[part, k], r_recv.at[part, source], device,
+        )
+
+    def g_copy(owner, part, k, device):
+        ref = result.at[pl.ds(pl.multiple_of(owner * tok_q, 16), tok_q), pl.ds(part * pw, pw)]
+        return remote(ref, ref, g_send.at[part, k], g_recv.at[part, owner], device)
+
+    def normalize(chunk):
+        cols = pl.ds(chunk * cw, cw)
+        hid = hidden[:, cols].astype(jnp.float32)
+        normed_ref[:, cols] = (
+            hid * inverse_wide * gain_ref[:, cols].astype(jnp.float32)
+        ).astype(jnp.bfloat16)
+
+    for chunk in range(CHUNKS // 2):
+        normalize(chunk)
+    for part in range(PARTS):
+        cols = pl.ds(part * pw, pw)
+        for source in range(n_dp):
+            p_copy(source, source, part, to_sib).wait_recv()
+        tokens[:, cols] = jnp.dot(
+            unplacer, returned[:, cols], preferred_element_type=jnp.float32
+        ).astype(jnp.bfloat16)
+        for k in (2, 1, 3):
+            to = lax.rem(tp + k, n_tp)
+            start(r_copy(to, tp, part, k, (sec, dp, to)))
+    for chunk in range(CHUNKS // 2, CHUNKS):
+        normalize(chunk)
+    mine_rows = pl.ds(pl.multiple_of(tp * tok_q, 16), tok_q)
+    for part in range(PARTS):
+        cols = pl.ds(part * pw, pw)
+        value = tokens[mine_rows, cols].astype(jnp.float32)
+        for k in range(1, n_tp):
+            who = lax.rem(tp + k, n_tp)
+            r_copy(tp, who, part, k, to_sib).wait_recv()
+            value = value + partial[who, :, cols].astype(jnp.float32)
+        result[mine_rows, cols] = value.astype(jnp.bfloat16)
+        for k in (2, 1, 3):
+            start(g_copy(tp, part, k, (sec, dp, lax.rem(tp + k, n_tp))))
+    for part in range(PARTS):
+        for k in range(1, n_tp):
+            g_copy(lax.rem(tp + k, n_tp), part, k, to_sib).wait_recv()
+    grad_ref[...] = result[...]
+    for copy in sent:
+        copy.wait_send()
+
+
+def kernel_body(feats, dest, proj_w, proj_b, text, gain, cot):
+    n_dp, n_tp = lax.axis_size("dp"), lax.axis_size("tp")
+    per_device, vision = feats.shape[1:]
+    rows, width = text.shape[1:]
+    quarter = rows // n_dp // n_tp
+    bf = jnp.bfloat16
+    dma = pltpu.SemaphoreType.DMA
+    vmem = pl.BlockSpec(memory_space=pltpu.VMEM)
+    hbm = pl.BlockSpec(memory_space=pl.ANY)
+    normed, feature_grad = pl.pallas_call(
+        kernel,
+        out_shape=(
+            jax.ShapeDtypeStruct((rows, width), bf),
+            jax.ShapeDtypeStruct((per_device, vision), bf),
+        ),
+        in_specs=[vmem, vmem, hbm, vmem, hbm, vmem, hbm],
+        out_specs=(vmem, vmem),
+        scratch_shapes=[
+            pltpu.VMEM((vision, width), bf),
+            pltpu.VMEM((rows, width), bf),
+            pltpu.VMEM((rows, width), bf),
+            pltpu.VMEM((n_dp, quarter, vision + FLAG), bf),
+            pltpu.VMEM((n_dp, n_tp, quarter, vision + FLAG), bf),
+            pltpu.VMEM((rows, width), bf),
+            pltpu.VMEM((rows, width), bf),
+            pltpu.VMEM((rows, vision), bf),
+            pltpu.VMEM((rows, vision), bf),
+            pltpu.VMEM((per_device, vision), bf),
+            pltpu.VMEM((n_tp, per_device // n_tp, vision), bf),
+            pltpu.VMEM((per_device, vision), bf),
+            pltpu.VMEM((n_tp, 8, rows), jnp.float32),
+            dma((3,)),
+            dma((CHUNKS, 8)),
+            dma((CHUNKS, 8)),
+            dma((n_dp,)),
+            dma((n_dp,)),
+            dma((n_tp,)),
+            dma((n_tp,)),
+            dma((n_tp,)),
+            dma((n_tp,)),
+            dma((PARTS, n_dp)),
+            dma((PARTS, n_dp)),
+            dma((PARTS, n_tp)),
+            dma((PARTS, n_tp)),
+            dma((PARTS, n_tp)),
+            dma((PARTS, n_tp)),
+        ],
+        compiler_params=pltpu.CompilerParams(
+            collective_id=0, has_side_effects=True, vmem_limit_bytes=44 * 1024 * 1024
+        ),
+    )(
+        feats[0], dest[0], proj_w, proj_b.reshape(1, width), text[0], gain.reshape(1, width), cot[0]
+    )
+    return normed[None], feature_grad[None]
+
+
 def solution(mesh):
     in_specs = (
         P("sec", "dp", None),
@@ -83,4 +390,5 @@
         P("sec", "dp", "tp"),
     )
     out_specs = (P("sec", "dp", "tp"), P("sec", "dp", None))
-    return jax.shard_map(body, mesh=mesh, in_specs=in_specs, out_specs=out_specs, check_vma=False)
+    small = mesh.shape["sec"] == 2 and mesh.shape["dp"] == 4 and mesh.shape["tp"] == 4
+    return jax.shard_map(kernel_body if small else body, mesh=mesh, in_specs=in_specs, out_specs=out_specs, check_vma=False)

time: 164 us -> 76.5 us (0.47)
  Pallas kernels: 0 us -> 67.1 us
  waiting for transfers between devices: 64.4 us -> 0 us
  blocking collectives: 59.9 us -> 0 us
  between operations: 14.2 us -> 0.66 us
  other arithmetic: 9.5 us -> 0 us
  matrix products: 7.98 us -> 0 us
  local copies, waits for them, and re-layouts: 1.02 us -> 8.33 us
  starting transfers between devices: 6.92 us -> 0 us
    pallas_call x0 -> x1, Pallas kernels: none -> 67.1 us  [kernel_body(): pl.pallas_call(kernel, out_shape=(jax.ShapeDtypeStruct((rows, width), bf)...]
    all_gather x1 -> x0, waiting for transfers between devices: 42.7 us -> none  [body(): weight = lax.all_gather(proj_w, ('sec', 'dp'), axis=0, tiled=True)]
    psum x2 -> x0, blocking collectives: 42.5 us -> none  [the longest x1 30.8 us: body(): feature_grad = lax.psum(partial_value, 'tp').astype(jnp.bfloat16)]
    all_to_all x1 -> x0, blocking collectives: 17.4 us -> none  [route_forward(): lax.all_to_all(outgoing, 'dp', split_axis=0, concat_axis=0, tiled=True)]
    all_to_all x2 -> x0, waiting for transfers between devices: 17.1 us -> none  [the longest x1 12.6 us: route_backward(): return lax.all_to_all(hopped, 'dp', split_axis=0, concat_axis=0, tiled=True)]
    unnamed x8 -> x16, local copies, waits for them, and re-layouts: 0.03 us -> 8.2 us
    dot_general x2 -> x0, matrix products: 7.98 us -> none  [the longest x1 4.37 us: body(): lax.dot_general(grad_tokens, weight, (((1,), (1,)), ((), ())), preferred_...]
    all_to_all x2 -> x0, starting transfers between devices: 6.74 us -> none  [the longest x1 3.52 us: route_backward(): return lax.all_to_all(hopped, 'dp', split_axis=0, concat_axis=0, tiled=True)]
  transfers between devices with their start and end apart: 6 -> 0, of which waited for: 5 -> 0; matrix products, arithmetic and copies ran while one was open for 3% -> 0% of each run, Pallas kernels for 0% -> 0%
where the time goes in v1:
time: 76.5 us; the launch traced here: 76.1 us
  Pallas kernels  67.1 us (88%)
  local copies, waits for them, and re-layouts  8.33 us (11%)
    pallas_call x1, Pallas kernels, kernel_body(): pl.pallas_call(kernel, out_shape=(jax.ShapeDtypeStruct((rows, width), bf)...  67.1 us
    unnamed x16, local copies, waits for them, and re-layouts  8.2 us

profile of v1, /device:TPU:0, one launch (start us, length us, event | category | flops | bytes accessed | tf_op | source)
XLA Modules:
  0.0 76.1 jit_solution(10575058021599839004)
XLA Ops:
  0.6 0.0 copy-start.4
  0.6 0.7 copy-done.4
  1.3 0.0 copy-start.5
  1.3 0.7 copy-done.5
  2.0 0.0 copy-start.6
  2.0 0.6 copy-done.6
  2.7 0.1 copy.9.dest_ref
  2.8 0.0 copy-start
  2.8 1.2 %copy-done = bf16[1,256,2048]{2,1,0:T(8,128)(2,1)S(1)} copy-done((bf16[1,256,2048]{2,1,0:T(8,128)(2,1)S(1)}, bf16[1,256,2048]{2,1,0:T(8,128)(2,1)}, u32[]{:S(2)}) %copy-start) | copy-done | bytes 1048600
  4.0 0.0 copy-start.1
  4.0 1.2 %copy-done.1 = bf16[1,256,2048]{2,1,0:T(8,128)(2,1)S(1)} copy-done((bf16[1,256,2048]{2,1,0:T(8,128)(2,1)S(1)}, bf16[1,256,2048]{2,1,0:T(8,128)(2,1)}, u32[]{:S(2)}) %copy-start.1) | copy-done | bytes 1048600
  5.2 0.0 copy-start.2
  5.2 1.1 %copy-done.2 = bf16[160,2048]{1,0:T(8,128)(2,1)S(1)} copy-done((bf16[160,2048]{1,0:T(8,128)(2,1)S(1)}, bf16[160,2048]{1,0:T(8,128)(2,1)}, u32[]{:S(2)}) %copy-start.2) | copy-done | bytes 655384
  6.3 0.0 copy-start.3
  6.3 1.0 %copy-done.3 = bf16[1,128,1280]{2,1,0:T(8,128)(2,1)S(1)} copy-done((bf16[1,128,1280]{2,1,0:T(8,128)(2,1)S(1)}, bf16[1,128,1280]{2,1,0:T(8,128)(2,1)}, u32[]{:S(2)}) %copy-start.3) | copy-done | bytes 327704
  7.3 67.1 %shard_map.86 = (bf16[256,2048]{1,0:T(8,128)(2,1)S(1)}, bf16[128,1280]{1,0:T(8,128)(2,1)S(1)}) custom-call(bf16[128,1280]{1,0:T(8,128)(2,1)S(1)} %bitcast.9, s32[128,1]{1,0:T(8,128)S(1)} %copy.9.dest_ref, bf16[160,2048]{1,0:T(8,128)(2,1)S(1)} %copy-done.2, bf16[1,2048]{1,0:T(2,128)(2,1)S(1)} %reshape.10.bias_ref, bf16[256,2048]{1,0:T(8,128)(2,1)S(1)} %bitcast.6, ...), custom_call_target="tpu_custom_call" | custom-call | tf_op jit(solution)/shard_map/pallas_call | solution.py:335
  74.4 1.0 %copy.12 = bf16[1,256,2048]{2,1,0:T(8,128)(2,1)} copy(bf16[1,256,2048]{2,1,0:T(8,128)(2,1)S(1)} %bitcast.8) | data formatting | bytes 2097152
  75.4 0.7 copy.13
  (2 shorter events, 0.0 us)
Async XLA Ops:
  0.6 0.7 copy-start.4
  1.3 0.7 copy-start.5
  2.0 0.7 copy-start.6
  2.8 1.2 %copy-start = (bf16[1,256,2048]{2,1,0:T(8,128)(2,1)S(1)}, bf16[1,256,2048]{2,1,0:T(8,128)(2,1)}, u32[]{:S(2)}) copy-start(bf16[1,256,2048]{2,1,0:T(8,128)(2,1)} %param.11) | copy-start | bytes 3145732
  4.0 1.2 %copy-start.1 = (bf16[1,256,2048]{2,1,0:T(8,128)(2,1)S(1)}, bf16[1,256,2048]{2,1,0:T(8,128)(2,1)}, u32[]{:S(2)}) copy-start(bf16[1,256,2048]{2,1,0:T(8,128)(2,1)} %param.13) | copy-start | bytes 3145732
  5.2 1.1 %copy-start.2 = (bf16[160,2048]{1,0:T(8,128)(2,1)S(1)}, bf16[160,2048]{1,0:T(8,128)(2,1)}, u32[]{:S(2)}) copy-start(bf16[160,2048]{1,0:T(8,128)(2,1)} %shard_ref.1) | copy-start | bytes 1966084
  6.3 1.0 %copy-start.3 = (bf16[1,128,1280]{2,1,0:T(8,128)(2,1)S(1)}, bf16[1,128,1280]{2,1,0:T(8,128)(2,1)}, u32[]{:S(2)}) copy-start(bf16[1,128,1280]{2,1,0:T(8,128)(2,1)} %param.7) | copy-start | bytes 983044

commit v2 on v1

--- a/solution.py
+++ b/solution.py
@@ -84,9 +84,9 @@
 
 
 def kernel(
-    feats_ref, dest_ref, shard_ref, bias_ref, text_hbm, gain_ref, cot_hbm,
+    feats_hbm, dest_ref, shard_hbm, bias_ref, text_hbm, gain_ref, cot_hbm,
     normed_ref, grad_ref,
-    weight, text, cot, outbox, slots, hidden, grad, product, returned, tokens, partial, result, stats,
+    feats, weight, text, cot, outbox, slots, hidden, grad, product, returned, tokens, partial, result, stats,
     local_sem, w_send, w_recv, x_send, x_recv, y_send, y_recv, s_send, s_recv,
     p_send, p_recv, r_send, r_recv, g_send, g_recv,
 ):
@@ -95,8 +95,8 @@
     x_dp = dp + 1 - 2 * lax.rem(dp, 2)
     y_dp = lax.rem(dp + 2, 4)
     d_dp = 3 - dp
-    per_device, vision = feats_ref.shape
-    depth, width = shard_ref.shape
+    per_device, vision = feats.shape
+    depth, width = shard_hbm.shape
     n_dp, n_tp, quarter, _ = slots.shape
     cap = n_tp * quarter
     rows = n_dp * cap
@@ -109,12 +109,18 @@
         return pl.multiple_of((sec_of * n_dp + dp_of) * depth, 16)
 
     own = block(sec, dp)
-    local = [
-        pltpu.make_async_copy(shard_ref, weight.at[pl.ds(own, depth)], local_sem.at[0]),
-        pltpu.make_async_copy(text_hbm, text, local_sem.at[1]),
-        pltpu.make_async_copy(cot_hbm, cot, local_sem.at[2]),
+    in_feats = pltpu.make_async_copy(feats_hbm, feats, local_sem.at[CHUNKS])
+    in_text = pltpu.make_async_copy(text_hbm, text, local_sem.at[CHUNKS + 1])
+    in_cot = pltpu.make_async_copy(cot_hbm, cot, local_sem.at[CHUNKS + 2])
+    in_shard = [
+        pltpu.make_async_copy(
+            shard_hbm.at[:, pl.ds(chunk * cw, cw)],
+            weight.at[chunk, pl.ds(own, depth)],
+            local_sem.at[chunk],
+        )
+        for chunk in range(CHUNKS)
     ]
-    for copy in local:
+    for copy in [in_feats, *in_shard, in_text, in_cot]:
         copy.start()
 
     barrier = pltpu.get_barrier_semaphore()
@@ -124,11 +130,44 @@
     for peer in peers:
         pl.semaphore_signal(barrier, inc=1, device_id=peer, device_id_type=MESH)
 
-    t_col = dest_ref[...].astype(jnp.float32)
+    def remote(src, dst, send, recv, device):
+        return pltpu.make_async_remote_copy(
+            src_ref=src, dst_ref=dst, send_sem=send, recv_sem=recv,
+            device_id=device, device_id_type=MESH,
+        )
+
+    sent = []
+
+    def start(copy):
+        copy.start()
+        sent.append(copy)
+
+    def w_copy(first, count, chunk, kind, device):
+        ref = weight.at[chunk, pl.ds(first, count)]
+        return remote(ref, ref, w_send.at[chunk, kind], w_recv.at[chunk, kind], device)
+
+    to_x, to_y, to_sib = (sec, x_dp, tp), (sec, y_dp, tp), (other, dp, tp)
+    jx, jy, jd = block(sec, x_dp), block(sec, y_dp), block(sec, d_dp)
+    jd_low = pl.multiple_of(jd + half, 16)
+    jy_low = pl.multiple_of(jy + half, 16)
+    sib = [block(other, k) for k in (dp, x_dp, y_dp, d_dp)]
+
+    def send_own(chunk):
+        in_shard[chunk].wait()
+        start(w_copy(own, depth, chunk, 0, to_x))
+        start(w_copy(own, depth, chunk, 1, to_y))
+        start(w_copy(own, depth, chunk, 4, to_sib))
+
+    pl.semaphore_wait(barrier, len(peers))
+
+    send_own(0)
+    send_own(1)
+
+    t_row = dest_ref[...].astype(jnp.float32)
     square = (per_device, per_device)
     down = lax.broadcasted_iota(jnp.int32, square, 0)
     along = lax.broadcasted_iota(jnp.int32, square, 1)
-    t_row = jnp.sum(jnp.where(down == along, t_col, 0.0), axis=0, keepdims=True)
+    t_col = jnp.sum(jnp.where(down == along, t_row, 0.0), axis=1, keepdims=True)
     same = t_col == t_row
     before_row = jnp.sum(jnp.where(same & (down < along), 1.0, 0.0), axis=0, keepdims=True)
     before_col = jnp.sum(jnp.where(same & (along < down), 1.0, 0.0), axis=1, keepdims=True)
@@ -138,46 +177,17 @@
     mine = mine + (mine // quarter) * (cap - quarter) + tp * quarter
     placer = jnp.where(mine == slot_row, 1.0, 0.0)
     filled = jnp.broadcast_to(jnp.sum(placer, axis=1, keepdims=True), (n_dp * quarter, FLAG))
-    routed = jnp.dot(placer.astype(jnp.bfloat16), feats_ref[...], preferred_element_type=jnp.float32)
+    in_feats.wait()
+    routed = jnp.dot(placer.astype(jnp.bfloat16), feats[...], preferred_element_type=jnp.float32)
     outbox[:, :, pl.ds(0, vision)] = routed.astype(jnp.bfloat16).reshape(n_dp, quarter, vision)
     outbox[:, :, pl.ds(vision, FLAG)] = filled.astype(jnp.bfloat16).reshape(n_dp, quarter, FLAG)
     unplacer = jnp.where(
         slot_col == lax.broadcasted_iota(jnp.int32, (per_device, rows), 1), 1.0, 0.0
     ).astype(jnp.bfloat16)
 
-    def remote(src, dst, send, recv, device):
-        return pltpu.make_async_remote_copy(
-            src_ref=src, dst_ref=dst, send_sem=send, recv_sem=recv,
-            device_id=device, device_id_type=MESH,
-        )
-
-    sent = []
-
-    def start(copy):
-        copy.start()
-        sent.append(copy)
-
-    def w_copy(first, count, chunk, kind, device):
-        ref = weight.at[pl.ds(first, count), pl.ds(chunk * cw, cw)]
-        return remote(ref, ref, w_send.at[chunk, kind], w_recv.at[chunk, kind], device)
-
-    to_x, to_y, to_sib = (sec, x_dp, tp), (sec, y_dp, tp), (other, dp, tp)
-    jx, jy, jd = block(sec, x_dp), block(sec, y_dp), block(sec, d_dp)
-    jd_low = pl.multiple_of(jd + half, 16)
-    jy_low = pl.multiple_of(jy + half, 16)
-    sib = [block(other, k) for k in (dp, x_dp, y_dp, d_dp)]
-
-    def send_own(chunk):
-        start(w_copy(own, depth, chunk, 0, to_x))
-        start(w_copy(own, depth, chunk, 1, to_y))
-        start(w_copy(own, depth, chunk, 4, to_sib))
-
-    local[0].wait()
-    pl.semaphore_wait(barrier, len(peers))
-
     for to in (d_dp, x_dp, y_dp, dp):
         start(remote(outbox.at[to], slots.at[dp, tp], x_send.at[to], x_recv.at[dp], (other, to, tp)))
-    for chunk in range(AHEAD):
+    for chunk in range(2, AHEAD):
         send_own(chunk)
     for source in range(n_dp):
         remote(outbox.at[source], slots.at[source, tp], x_send.at[source], x_recv.at[source], to_sib).wait_recv()
@@ -189,7 +199,7 @@
         cols = pl.ds(chunk * cw, cw)
         value = jnp.dot(
             slots[:, :, :, pl.ds(0, vision)].reshape(rows, vision),
-            weight[:, cols],
+            weight[chunk],
             preferred_element_type=jnp.float32,
         )
         value = (value + bias_ref[:, cols].astype(jnp.float32)).astype(jnp.bfloat16)
@@ -206,6 +216,11 @@
 
     square_sum = jnp.zeros((rows, 128), jnp.float32)
     cross_sum = jnp.zeros((rows, 128), jnp.float32)
+    ready = {
+        CHUNKS - 1: range(CHUNKS // 2 - 1),
+        CHUNKS: range(CHUNKS // 2 - 1, CHUNKS - 1),
+        CHUNKS + 1: (CHUNKS - 1,),
+    }
     for step in range(CHUNKS + 2):
         if step < CHUNKS:
             w_copy(jx, depth, step, 0, to_x).wait_recv()
@@ -220,16 +235,16 @@
             w_copy(jd, half, step - 1, 2, to_y).wait_recv()
             w_copy(jd_low, half, step - 1, 3, to_x).wait_recv()
             start(w_copy(jd, depth, step - 1, 7, to_sib))
-        if step == 2:
+        if step == CHUNKS - 1:
             for k in range(1, n_tp):
                 who = lax.rem(tp + k, n_tp)
                 remote(slots.at[:, who], slots.at[:, who], y_send.at[k], y_recv.at[who], to_sib).wait_recv()
-            local[1].wait()
-            local[2].wait()
-        if step >= 2:
+            in_text.wait()
+            in_cot.wait()
+        for chunk in ready.get(step, ()):
             for kind in range(4):
-                w_copy(sib[kind], depth, step - 2, 4 + kind, to_sib).wait_recv()
-            square_sum, cross_sum = project(step - 2, square_sum, cross_sum)
+                w_copy(sib[kind], depth, chunk, 4 + kind, to_sib).wait_recv()
+            square_sum, cross_sum = project(chunk, square_sum, cross_sum)
 
     stats[tp, pl.ds(0, 1), :] = jnp.sum(square_sum.T, axis=0, keepdims=True)
     stats[tp, pl.ds(1, 1), :] = jnp.sum(cross_sum.T, axis=0, keepdims=True)
@@ -255,32 +270,32 @@
         grad[:, cols] = (inverse_wide * scaled - hid * factor_wide).astype(jnp.bfloat16)
 
     def p_copy(source, to, part, device):
-        cols = pl.ds(part * pw, pw)
         return remote(
-            product.at[pl.ds(pl.multiple_of(to * cap, 16), cap), cols],
-            returned.at[pl.ds(pl.multiple_of(source * cap, 16), cap), cols],
+            product.at[part, pl.ds(pl.multiple_of(to * cap, 16), cap)],
+            returned.at[part, pl.ds(pl.multiple_of(source * cap, 16), cap)],
             p_send.at[part, to], p_recv.at[part, source], device,
         )
 
     for part in range(PARTS):
-        value = lax.dot_general(
-            grad[...], weight[pl.ds(part * pw, pw), :], (((1,), (1,)), ((), ())),
-            preferred_element_type=jnp.float32,
-        )
-        product[:, pl.ds(part * pw, pw)] = value.astype(jnp.bfloat16)
+        value = jnp.zeros((rows, pw), jnp.float32)
+        for chunk in range(CHUNKS):
+            value = value + lax.dot_general(
+                grad[:, pl.ds(chunk * cw, cw)], weight[chunk, pl.ds(part * pw, pw), :],
+                (((1,), (1,)), ((), ())), preferred_element_type=jnp.float32,
+            )
+        product[part] = value.astype(jnp.bfloat16)
         for to in (d_dp, x_dp, y_dp, dp):
             start(p_copy(dp, to, part, (other, to, tp)))
 
     def r_copy(owner, source, part, k, device):
-        cols = pl.ds(part * pw, pw)
         return remote(
-            tokens.at[pl.ds(pl.multiple_of(owner * tok_q, 16), tok_q), cols],
-            partial.at[source, :, cols],
+            tokens.at[part, pl.ds(pl.multiple_of(owner * tok_q, 16), tok_q)],
+            partial.at[part, source],
             r_send.at[part, k], r_recv.at[part, source], device,
         )
 
     def g_copy(owner, part, k, device):
-        ref = result.at[pl.ds(pl.multiple_of(owner * tok_q, 16), tok_q), pl.ds(part * pw, pw)]
+        ref = result.at[part, pl.ds(pl.multiple_of(owner * tok_q, 16), tok_q)]
         return remote(ref, ref, g_send.at[part, k], g_recv.at[part, owner], device)
 
     def normalize(chunk):
@@ -293,11 +308,10 @@
     for chunk in range(CHUNKS // 2):
         normalize(chunk)
     for part in range(PARTS):
-        cols = pl.ds(part * pw, pw)
         for source in range(n_dp):
             p_copy(source, source, part, to_sib).wait_recv()
-        tokens[:, cols] = jnp.dot(
-            unplacer, returned[:, cols], preferred_element_type=jnp.float32
+        tokens[part] = jnp.dot(
+            unplacer, returned[part], preferred_element_type=jnp.float32
         ).astype(jnp.bfloat16)
         for k in (2, 1, 3):
             to = lax.rem(tp + k, n_tp)
@@ -306,19 +320,18 @@
         normalize(chunk)
     mine_rows = pl.ds(pl.multiple_of(tp * tok_q, 16), tok_q)
     for part in range(PARTS):
-        cols = pl.ds(part * pw, pw)
-        value = tokens[mine_rows, cols].astype(jnp.float32)
+        value = tokens[part, mine_rows].astype(jnp.float32)
         for k in range(1, n_tp):
             who = lax.rem(tp + k, n_tp)
             r_copy(tp, who, part, k, to_sib).wait_recv()
-            value = value + partial[who, :, cols].astype(jnp.float32)
-        result[mine_rows, cols] = value.astype(jnp.bfloat16)
+            value = value + partial[part, who].astype(jnp.float32)
+        result[part, mine_rows] = value.astype(jnp.bfloat16)
         for k in (2, 1, 3):
             start(g_copy(tp, part, k, (sec, dp, lax.rem(tp + k, n_tp))))
     for part in range(PARTS):
         for k in range(1, n_tp):
             g_copy(lax.rem(tp + k, n_tp), part, k, to_sib).wait_recv()
-    grad_ref[...] = result[...]
+        grad_ref[:, pl.ds(part * pw, pw)] = result[part]
     for copy in sent:
         copy.wait_send()
 
@@ -331,30 +344,31 @@
     bf = jnp.bfloat16
     dma = pltpu.SemaphoreType.DMA
     vmem = pl.BlockSpec(memory_space=pltpu.VMEM)
-    hbm = pl.BlockSpec(memory_space=pl.ANY)
+    hbm = pl.BlockSpec(memory_space=pltpu.HBM)
     normed, feature_grad = pl.pallas_call(
         kernel,
         out_shape=(
             jax.ShapeDtypeStruct((rows, width), bf),
             jax.ShapeDtypeStruct((per_device, vision), bf),
         ),
-        in_specs=[vmem, vmem, hbm, vmem, hbm, vmem, hbm],
+        in_specs=[hbm, vmem, hbm, vmem, hbm, vmem, hbm],
         out_specs=(vmem, vmem),
         scratch_shapes=[
-            pltpu.VMEM((vision, width), bf),
+            pltpu.VMEM((per_device, vision), bf),
+            pltpu.VMEM((CHUNKS, vision, width // CHUNKS), bf),
             pltpu.VMEM((rows, width), bf),
             pltpu.VMEM((rows, width), bf),
             pltpu.VMEM((n_dp, quarter, vision + FLAG), bf),
             pltpu.VMEM((n_dp, n_tp, quarter, vision + FLAG), bf),
             pltpu.VMEM((rows, width), bf),
             pltpu.VMEM((rows, width), bf),
-            pltpu.VMEM((rows, vision), bf),
-            pltpu.VMEM((rows, vision), bf),
-            pltpu.VMEM((per_device, vision), bf),
-            pltpu.VMEM((n_tp, per_device // n_tp, vision), bf),
-            pltpu.VMEM((per_device, vision), bf),
+            pltpu.VMEM((PARTS, rows, vision // PARTS), bf),
+            pltpu.VMEM((PARTS, rows, vision // PARTS), bf),
+            pltpu.VMEM((PARTS, per_device, vision // PARTS), bf),
+            pltpu.VMEM((PARTS, n_tp, per_device // n_tp, vision // PARTS), bf),
+            pltpu.VMEM((PARTS, per_device, vision // PARTS), bf),
             pltpu.VMEM((n_tp, 8, rows), jnp.float32),
-            dma((3,)),
+            dma((CHUNKS + 3,)),
             dma((CHUNKS, 8)),
             dma((CHUNKS, 8)),
             dma((n_dp,)),
@@ -371,10 +385,10 @@
             dma((PARTS, n_tp)),
         ],
         compiler_params=pltpu.CompilerParams(
-            collective_id=0, has_side_effects=True, vmem_limit_bytes=44 * 1024 * 1024
+            collective_id=0, has_side_effects=True, vmem_limit_bytes=63 * 1024 * 1024
         ),
     )(
-        feats[0], dest[0], proj_w, proj_b.reshape(1, width), text[0], gain.reshape(1, width), cot[0]
+        feats[0], dest.reshape(1, per_device), proj_w, proj_b.reshape(1, width), text[0], gain.reshape(1, width), cot[0]
     )
     return normed[None], feature_grad[None]
 

time: 76.5 us -> 68.1 us (0.89)
  Pallas kernels: 67.1 us -> 62 us
  local copies, waits for them, and re-layouts: 8.33 us -> 5.05 us
    pallas_call x1, Pallas kernels: 67.1 us -> 62 us  [kernel_body(): pl.pallas_call(kernel, out_shape=(jax.ShapeDtypeStruct((rows, width), bf)...]
    unnamed x16 -> x8, local copies, waits for them, and re-layouts: 8.2 us -> 3.85 us
where the time goes in v2:
time: 68.1 us; the launch traced here: 67.7 us
  Pallas kernels  62 us (91%)
  local copies, waits for them, and re-layouts  5.05 us (7%)
    pallas_call x1, Pallas kernels, kernel_body(): pl.pallas_call(kernel, out_shape=(jax.ShapeDtypeStruct((rows, width), bf)...  62 us
    unnamed x8, local copies, waits for them, and re-layouts  3.85 us

profile of v2, /device:TPU:0, one launch (start us, length us, event | category | flops | bytes accessed | tf_op | source)
XLA Modules:
  0.0 67.7 jit_solution(12788639932849848282)
XLA Ops:
  0.6 0.0 copy-start.1
  0.6 0.7 %copy-done.1 = bf16[2048]{0:T(1024)(128)(2,1)S(1)} copy-done((bf16[2048]{0:T(1024)(128)(2,1)S(1)}, bf16[2048]{0:T(1024)(128)(2,1)}, u32[]{:S(2)}) %copy-start.1) | copy-done | bytes 4120
  1.3 0.0 copy-start.2
  1.3 0.6 reshape.14.bias_ref
  1.9 0.1 copy-done.2
  2.0 0.6 reshape.15.gain_ref
  2.6 62.0 %shard_map.86 = (bf16[256,2048]{1,0:T(8,128)(2,1)}, bf16[128,1280]{1,0:T(8,128)(2,1)}) custom-call(bf16[128,1280]{1,0:T(8,128)(2,1)} %bitcast.9, s32[1,128]{1,0:T(1,128)} %bitcast.11, bf16[160,2048]{1,0:T(8,128)(2,1)} %shard_hbm.1, bf16[1,2048]{1,0:T(2,128)(2,1)} %reshape.14.bias_ref, bf16[256,2048]{1,0:T(8,128)(2,1)} %bitcast.6, ...), custom_call_target="tpu_custom_call" | custom-call | tf_op jit(solution)/shard_map/pallas_call | solution.py:348
  64.6 0.0 copy-start
  64.6 2.4 %copy.11 = bf16[1,256,2048]{2,1,0:T(8,128)(2,1)} copy(bf16[1,256,2048]{2,1,0:T(8,128)(2,1)} %bitcast.8) | data formatting | bytes 2097152
  66.9 0.0 copy-done
  66.9 0.7 %copy.12 = bf16[1,128,1280]{2,1,0:T(8,128)(2,1)} copy(bf16[1,128,1280]{2,1,0:T(8,128)(2,1)S(1)} %bitcast.10) | data formatting | bytes 655360
Async XLA Ops:
  0.6 0.7 %copy-start.1 = (bf16[2048]{0:T(1024)(128)(2,1)S(1)}, bf16[2048]{0:T(1024)(128)(2,1)}, u32[]{:S(2)}) copy-start(bf16[2048]{0:T(1024)(128)(2,1)} %param.10) | copy-start | bytes 12292
  1.3 0.7 %copy-start.2 = (bf16[2048]{0:T(1024)(128)(2,1)S(1)}, bf16[2048]{0:T(1024)(128)(2,1)}, u32[]{:S(2)}) copy-start(bf16[2048]{0:T(1024)(128)(2,1)} %param.12) | copy-start | bytes 12292
  64.6 2.4 %copy-start = (bf16[128,1280]{1,0:T(8,128)(2,1)S(1)}, bf16[128,1280]{1,0:T(8,128)(2,1)}, u32[]{:S(2)}) copy-start(bf16[128,1280]{1,0:T(8,128)(2,1)} %get-tuple-element.5) | copy-start | bytes 983044

commit v3 on v2

--- a/solution.py
+++ b/solution.py
@@ -202,12 +202,12 @@
             weight[chunk],
             preferred_element_type=jnp.float32,
         )
-        value = (value + bias_ref[:, cols].astype(jnp.float32)).astype(jnp.bfloat16)
+        value = (value + bias_ref[cols].astype(jnp.float32).reshape(1, cw)).astype(jnp.bfloat16)
         flag = slots[:, :, :, pl.ds(vision, FLAG)].reshape(rows, FLAG).astype(jnp.float32)
         flag = jnp.concatenate([flag] * (cw // FLAG), axis=1)
         hid = jnp.where(flag > 0.5, value.astype(jnp.float32), text[:, cols].astype(jnp.float32))
         hidden[:, cols] = hid.astype(jnp.bfloat16)
-        scaled = cot[:, cols].astype(jnp.float32) * gain_ref[:, cols].astype(jnp.float32)
+        scaled = cot[:, cols].astype(jnp.float32) * gain_ref[cols].astype(jnp.float32).reshape(1, cw)
         for first in range(0, cw, 128):
             part = hid[:, first:first + 128]
             square_sum = square_sum + part * part
@@ -265,7 +265,7 @@
 
     for chunk in range(CHUNKS):
         cols = pl.ds(chunk * cw, cw)
-        scaled = cot[:, cols].astype(jnp.float32) * gain_ref[:, cols].astype(jnp.float32)
+        scaled = cot[:, cols].astype(jnp.float32) * gain_ref[cols].astype(jnp.float32).reshape(1, cw)
         hid = hidden[:, cols].astype(jnp.float32)
         grad[:, cols] = (inverse_wide * scaled - hid * factor_wide).astype(jnp.bfloat16)
 
@@ -302,7 +302,7 @@
         cols = pl.ds(chunk * cw, cw)
         hid = hidden[:, cols].astype(jnp.float32)
         normed_ref[:, cols] = (
-            hid * inverse_wide * gain_ref[:, cols].astype(jnp.float32)
+            hid * inverse_wide * gain_ref[cols].astype(jnp.float32).reshape(1, cw)
         ).astype(jnp.bfloat16)
 
     for chunk in range(CHUNKS // 2):
@@ -388,7 +388,7 @@
             collective_id=0, has_side_effects=True, vmem_limit_bytes=63 * 1024 * 1024
         ),
     )(
-        feats[0], dest.reshape(1, per_device), proj_w, proj_b.reshape(1, width), text[0], gain.reshape(1, width), cot[0]
+        feats[0], dest.reshape(1, per_device), proj_w, proj_b, text[0], gain, cot[0]
     )
     return normed[None], feature_grad[None]
 

time: 68.1 us -> 66 us (0.969)
  local copies, waits for them, and re-layouts: 5.05 us -> 3.08 us
    reshape x2 -> x0, local copies, waits for them, and re-layouts: 1.21 us -> none  [the longest x1 0.6 us: kernel_body(): proj_b.reshape(1, width)]
    unnamed x8 -> x4, local copies, waits for them, and re-layouts: 3.85 us -> 3.08 us
where the time goes in v3:
time: 66 us; the launch traced here: 65.7 us
  Pallas kernels  62 us (94%)
  local copies, waits for them, and re-layouts  3.08 us (5%)
    pallas_call x1, Pallas kernels, kernel_body(): pl.pallas_call(kernel, out_shape=(jax.ShapeDtypeStruct((rows, width), bf)...  62 us
    unnamed x4, local copies, waits for them, and re-layouts  3.08 us

profile of v3, /device:TPU:0, one launch (start us, length us, event | category | flops | bytes accessed | tf_op | source)
XLA Modules:
  0.0 65.7 jit_solution(10994215654239674860)
XLA Ops:
  0.6 62.0 %shard_map.86 = (bf16[256,2048]{1,0:T(8,128)(2,1)}, bf16[128,1280]{1,0:T(8,128)(2,1)}) custom-call(bf16[128,1280]{1,0:T(8,128)(2,1)} %bitcast.9, s32[1,128]{1,0:T(1,128)} %bitcast.11, bf16[160,2048]{1,0:T(8,128)(2,1)} %shard_hbm.1, bf16[2048]{0:T(1024)(128)(2,1)} %bias_ref.1, bf16[256,2048]{1,0:T(8,128)(2,1)} %bitcast.6, bf16[2048]{0:T(1024)(128)(2,1)} %gain_ref.1, ...), custom_call_target="tpu_custom_call" | custom-call | tf_op jit(solution)/shard_map/pallas_call | solution.py:348
  62.6 0.0 copy-start
  62.6 2.4 %copy.11 = bf16[1,256,2048]{2,1,0:T(8,128)(2,1)} copy(bf16[1,256,2048]{2,1,0:T(8,128)(2,1)} %bitcast.8) | data formatting | bytes 2097152
  65.0 0.0 copy-done
  65.0 0.7 %copy.12 = bf16[1,128,1280]{2,1,0:T(8,128)(2,1)} copy(bf16[1,128,1280]{2,1,0:T(8,128)(2,1)S(1)} %bitcast.10) | data formatting | bytes 655360
Async XLA Ops:
  62.6 2.4 %copy-start = (bf16[128,1280]{1,0:T(8,128)(2,1)S(1)}, bf16[128,1280]{1,0:T(8,128)(2,1)}, u32[]{:S(2)}) copy-start(bf16[128,1280]{1,0:T(8,128)(2,1)} %get-tuple-element.5) | copy-start | bytes 983044
